TPU v7x, 256 devices: a whole 4x4x8 slice. The times are simulated.
256 devices in a mesh: section: 8 (over z), tensor: 4 (over y), dp: 8 (over x, core).
Axes of the slice: x: 4, y: 4, z: 8, core: 2. Of those that a mesh axis runs over, the one named last changes fastest.
Arguments:
- hidden: bfloat16 [896, 5376], P('dp', ('section', 'tensor')), may hold values from -6 to 6
- head_weight: bfloat16 [5376, 131072], P(None, ('section', 'tensor', 'dp')), may hold values from -0.24549513 to 0.24549513
- targets: int32 [896], replicated, may hold values from 0 to 131071
- response_mask: int32 [896], replicated, may hold values from 0 to 1, as said below
- pair_ids: int32 [16], replicated, may hold values from 0 to 7, as said below
- ref_logprobs: float32 [16], replicated, may hold values from -3 to 3
Outputs:
- logprobs: float32 [16], replicated
- grad_hidden: bfloat16 [896, 5376], P('dp', ('section', 'tensor'))
- grad_weight: bfloat16 [5376, 131072], P(None, ('section', 'tensor', 'dp'))
Inputs may be any that keep to these rules, and one draw needn't show every extreme that they name: `pair_ids`: each pair id 0 to 7 names exactly two sequences. `response_mask`: in each sequence the ones form a suffix of at least 28 positions.
All inputs are finite; a program needn't handle non-finite values.
Results may differ from a plain program's by a relative error of at most 0.0046.
Values may be sent and summed in bfloat16 or wider, within the bound.
A program may use at most 128 MiB of HBM per device.

v0:
```python
import jax
import jax.numpy as jnp
from jax import lax
from jax.sharding import PartitionSpec as P

loss_scale = 2048.0
beta_value = 2.0


def pair_coefficients(logprobs, ref_logprobs, pair_ids):
    same = pair_ids[:, None] == pair_ids[None, :]
    order = jnp.arange(pair_ids.shape[0], dtype=jnp.int32)
    earlier = jnp.sum((same & (order[None, :] < order[:, None])).astype(jnp.int32), axis=1)
    signs = jnp.where(earlier == 0, 1.0, -1.0).astype(jnp.float32)
    contrib = signs * (logprobs - ref_logprobs)
    margin = jnp.sum(jnp.where(same, contrib[None, :], 0.0), axis=1)
    return -loss_scale * beta_value * jax.nn.sigmoid(-beta_value * margin) * signs


def per_device(hidden, head_weight, targets, response_mask, pair_ids, ref_logprobs):
    vocab_cols = head_weight.shape[1]
    seq_count = pair_ids.shape[0]
    seq_len = targets.shape[0] // seq_count
    partial_value = lax.all_gather(hidden, "dp", axis=0, tiled=True)
    gathered = lax.all_gather(partial_value, ("section", "tensor"), axis=1, tiled=True)
    logits = jnp.dot(gathered, head_weight, preferred_element_type=jnp.float32)
    first_col = lax.axis_index(("section", "tensor", "dp")) * vocab_cols
    columns = first_col + lax.broadcasted_iota(jnp.int32, (1, vocab_cols), 1)
    is_target = targets[:, None] == columns
    picked = jnp.sum(jnp.where(is_target, logits, 0.0), axis=1)
    local_top = jnp.max(logits, axis=1)
    row_top = lax.pmax(local_top, ("section", "tensor", "dp"))
    local_total = jnp.sum(jnp.exp(logits - row_top[:, None]), axis=1)
    row_total, target_logit = lax.psum((local_total, picked), ("section", "tensor", "dp"))
    log_total = row_top + jnp.log(row_total)
    mask_float = response_mask.astype(jnp.float32)
    counts = jnp.sum(mask_float.reshape(seq_count, seq_len), axis=1)
    token_terms = (target_logit - log_total) * mask_float
    logprobs = jnp.sum(token_terms.reshape(seq_count, seq_len), axis=1) / counts
    coefficient = pair_coefficients(logprobs, ref_logprobs, pair_ids)
    token_weight = jnp.repeat(coefficient / counts, seq_len) * mask_float
    probs = jnp.exp(logits - log_total[:, None])
    dlogits = (token_weight[:, None] * (is_target.astype(jnp.float32) - probs)).astype(jnp.bfloat16)
    grad_weight = lax.dot_general(
        gathered, dlogits, (((0,), (0,)), ((), ())), preferred_element_type=jnp.float32
    ).astype(jnp.bfloat16)
    grad_terms = lax.dot_general(
        dlogits, head_weight, (((1,), (1,)), ((), ())), preferred_element_type=jnp.float32
    )
    feature_sums = lax.psum_scatter(
        grad_terms, ("section", "tensor"), scatter_dimension=1, tiled=True
    )
    grad_hidden = lax.psum_scatter(feature_sums, "dp", scatter_dimension=0, tiled=True)
    return (logprobs, grad_hidden.astype(jnp.bfloat16), grad_weight)


def solution(mesh):
    placed = (
        P("dp", ("section", "tensor")),
        P(None, ("section", "tensor", "dp")),
        P(),
        P(),
        P(),
        P(),
    )
    return jax.shard_map(
        per_device,
        mesh=mesh,
        in_specs=placed,
        out_specs=(P(), P("dp", ("section", "tensor")), P(None, ("section", "tensor", "dp"))),
        check_vma=False,
    )
```

profile of v0, /device:TPU:8, one launch (start us, length us, event | category | flops | bytes accessed | tf_op | source)
XLA Modules:
  0.0 592.9 jit_solution(11755776108813908051)
XLA Ops:
  7.2 0.0 copy-start
  7.2 0.0 copy-start.2
  7.2 0.0 all-gather.3.cloned.1.call-start
  7.2 13.5 %all-gather = bf16[8,112,168]{1,2,0:T(8,128)(2,1)S(1)} all-gather(bf16[1,112,168]{1,2,0:T(8,128)(2,1)} %bitcast.11), channel_id=1, replica_groups=mesh['section'=8,'tensor'=4,'dp'=8] {'dp'}, dimensions={0}, use_global_device_ids=true | all-gather | bytes 338688 | tf_op jit(solution)/shard_map/all_gather | solution.py:24
  20.8 1.0 reshape.31
  21.8 0.0 all-gather.3.cloned.1.call-update
  21.8 0.0 reduce-scatter.9.cloned.1.call-start
  21.9 0.0 copy-done
  21.9 0.1 reshape.28
  22.0 0.1 reduce_sum.57
  22.1 0.0 copy-done.2
  22.1 0.2 convert_reduce_fusion
  22.3 0.0 copy-start.1
  22.3 105.3 %all-gather.3.cloned.1.call-done = bf16[896,5376]{0,1:T(8,128)(2,1)} async-done(((bf16[896,168]{0,1:T(8,128)(2,1)}), bf16[896,5376]{0,1:T(8,128)(2,1)}) %all-gather.3.cloned.1.call-update) | async-done | bytes 9633808 | tf_op jit(solution)/shard_map/all_gather | solution.py:25
  127.6 10.6 %fusion.9 = (f32[896]{0:T(1024)S(1)}, f32[896,512]{0,1:T(8,128)S(1)}) fusion(bf16[896,5376]{0,1:T(8,128)(2,1)} %all-gather.3.cloned.1.call-done, bf16[5376,512]{1,0:T(8,128)(2,1)} %param.7), kind=kOutput, calls=%fused_computation.22 | convolution fusion | flops 4932959232 | bytes 16977408 | tf_op jit(solution)/shard_map/dot_general | solution.py:26
  138.2 0.0 copy-start.3
  138.2 75.2 %pmax.7 = f32[896]{0:T(1024)S(1)} all-reduce(f32[896]{0:T(1024)S(1)} %get-tuple-element.23), channel_id=1, replica_groups=mesh['section'=8,'tensor'=4,'dp'=8] {'section','tensor','dp'}, use_global_device_ids=true, to_apply=%region_3.4 | all-reduce | flops 896 | bytes 7168 | tf_op jit(solution)/shard_map/pmax | solution.py:32
  213.4 0.0 copy-done.1
  213.4 0.4 exponential_reduce_fusion
  213.9 73.5 %all-reduce.1 = (f32[896]{0:T(1024)S(1)}, f32[896]{0:T(1024)S(1)}) all-reduce(f32[896]{0:T(1024)S(1)} %get-tuple-element.16, f32[896]{0:T(1024)S(1)} %get-tuple-element.15), channel_id=1, replica_groups=mesh['section'=8,'tensor'=4,'dp'=8] {'section','tensor','dp'}, use_global_device_ids=true, to_apply=%region_1.2 | all-reduce | flops 1792 | bytes 14336 | tf_op jit(solution)/shard_map/psum | solution.py:34
  287.3 0.1 reshape.27
  287.4 0.1 reduce_sum.56
  287.5 0.0 copy-done.3
  287.5 0.5 subtract_multiply_fusion.1
  288.0 0.2 fusion.5
  288.2 0.1 broadcast_in_dim.38
  288.3 0.1 reshape.29
  288.4 12.3 %fusion.7 = f32[896,5376]{0,1:T(8,128)} fusion(bf16[5376,512]{1,0:T(8,128)(2,1)} %param.7, f32[896,512]{0,1:T(8,128)S(1)} %get-tuple-element.24, f32[896]{0:T(1024)S(1)} %get-tuple-element.22, f32[896]{0:T(1024)S(1)} %convert_multiply_fusion, s32[896]{0:T(1024)S(1)} %copy-done.1, s32[512]{0:T(512)S(1)} %iota_add_fusion), kind=kOutput, calls=%fused_computation.21 | convolution fusion | flops 4935254016 | bytes 26620416 | tf_op jit(solution)/shard_map/dot_general | solution.py:47
  300.8 0.0 reduce-scatter.9.cloned.1.call-update
  300.8 0.2 reduce-scatter.7.cloned.1.call-start
  301.0 247.9 %reduce-scatter.9.cloned.1.call-done = f32[896,168]{0,1:T(8,128)} async-done(((f32[896,5376]{0,1:T(8,128)}), f32[896,168]{0,1:T(8,128)}) %reduce-scatter.9.cloned.1.call-update) | async-done | bytes 602128
  548.9 2.3 copy.16
  551.2 0.0 reduce-scatter.7.cloned.1.call-update
  551.2 11.8 %fusion = bf16[5376,512]{0,1:T(8,128)(2,1)} fusion(bf16[896,5376]{0,1:T(8,128)(2,1)} %all-gather.3.cloned.1.call-done, f32[896,512]{0,1:T(8,128)S(1)} %get-tuple-element.24, f32[896]{0:T(1024)S(1)} %get-tuple-element.22, f32[896]{0:T(1024)S(1)} %convert_multiply_fusion, s32[896]{0:T(1024)S(1)} %copy-done.1, s32[512]{0:T(512)S(1)} %iota_add_fusion), kind=kOutput, calls=%fused_computation.1 | convolution fusion | flops 4938006528 | bytes 16986624 | tf_op jit(solution)/shard_map/dot_general | solution.py:44
  563.0 8.3 %copy.15 = bf16[5376,512]{1,0:T(8,128)(2,1)} copy(bf16[5376,512]{0,1:T(8,128)(2,1)} %fusion) | data formatting | bytes 11010048
  571.3 13.5 %reduce-scatter.7.cloned.1.call-done = f32[112,168]{1,0:T(8,128)} async-done(((f32[896,168]{1,0:T(8,128)}), f32[112,168]{1,0:T(8,128)}) %reduce-scatter.7.cloned.1.call-update) | async-done | bytes 75280
  584.8 1.6 copy.17
  (6 shorter events, 0.1 us)
Async XLA Ops:
  7.2 14.7 %copy-start = (s32[896]{0:T(1024)S(1)}, s32[896]{0:T(1024)}, u32[]{:S(2)}) copy-start(s32[896]{0:T(1024)} %param.9) | copy-start | bytes 10756
  7.2 14.9 %copy-start.2 = (s32[16]{0:T(128)S(1)}, s32[16]{0:T(128)}, u32[]{:S(2)}) copy-start(s32[16]{0:T(128)} %param.10) | copy-start | bytes 196
  7.2 120.4 %all-gather.3.cloned.1.call-start = ((), (), s32[]{:S(2)}) async-start(), calls=%async_computation.2 | async-start | bytes 9934848 | tf_op jit(solution)/shard_map/all_gather | solution.py:25
  21.8 527.1 %reduce-scatter.9.cloned.1.call-start = ((), (), s32[]{:S(2)}) async-start(), calls=%async_computation.4 | async-start | bytes 19869696
  22.3 191.1 %copy-start.1 = (s32[896]{0:T(1024)S(1)}, s32[896]{0:T(1024)}, u32[]{:S(2)}) copy-start(s32[896]{0:T(1024)} %param.8) | copy-start | bytes 10756
  138.2 149.3 %copy-start.3 = (f32[16]{0:T(128)S(1)}, f32[16]{0:T(128)}, u32[]{:S(2)}) copy-start(f32[16]{0:T(128)} %param.11) | copy-start | bytes 196
  300.8 284.0 %reduce-scatter.7.cloned.1.call-start = ((), (), s32[]{:S(2)}) async-start(), calls=%async_computation.3 | async-start | bytes 1032192
Sparse Core Ops, SparseCore 0:
  21.9 105.6 all-gather.2
  300.9 247.9 reduce-scatter.8
  551.4 33.2 reduce-scatter.6
where the time goes:
time: 593 us
  waiting for transfers between devices  367 us (62%)
  blocking collectives  162 us (27%)
  matrix products  34.8 us (6%)
  between operations  13.9 us (2%)
  local copies, waits for them, and re-layouts  13.6 us (2%)
    unnamed x5, waiting for transfers between devices  261 us
    all_gather x1, waiting for transfers between devices, per_device(): lax.all_gather(partial_value, ('section', 'tensor'), axis=1, tiled=True)  105 us
    pmax x1, blocking collectives, per_device(): row_top = lax.pmax(local_top, ('section', 'tensor', 'dp'))  75.2 us
    psum x1, blocking collectives, per_device(): lax.psum((local_total, picked), ('section', 'tensor', 'dp'))  73.5 us
    all_gather x1, blocking collectives, per_device(): partial_value = lax.all_gather(hidden, 'dp', axis=0, tiled=True)  13.5 us
    unnamed x12, local copies, waits for them, and re-layouts  13.2 us
    dot_general x1, matrix products, per_device(): lax.dot_general(dlogits, head_weight, (((1,), (1,)), ((), ())), preferred...  12.3 us
  transfers between devices with their start and end apart: 3, of which 3 were waited for; matrix products, arithmetic and copies ran while one was open for 3% of the time, Pallas kernels for 0%

commit v1 on v0

v1 whole, which is shorter than its diff:
```python
import jax
import jax.numpy as jnp
from jax import lax
from jax.experimental import pallas as pl
from jax.experimental.pallas import tpu as pltpu
from jax.sharding import PartitionSpec as P

loss_scale = 2048.0
beta_value = 2.0

MESH = pl.DeviceIdType.MESH
SIZE = {"z": 8, "y": 4, "x": 4}
BLOB = 11
PARTS = (
    (0, 4, ("y", "z", "x")),
    (4, 8, ("z", "x", "y")),
    (8, 11, ("x", "y", "z")),
)
LANES = 128
TILE = 16
ROWS = 112
TOK = 896
COLS = 512
PAIRS = 16
PAIR = 336
PADDED = 384
F32 = jnp.float32
BF16 = jnp.bfloat16
STEP_US = 1.5
GBS = 45.0e3


def whole(index):
    return slice(None) if index is None else index


class Comm:
    def __init__(self, send_sem, recv_sem):
        self.z = lax.axis_index("section")
        self.y = lax.axis_index("tensor")
        dp = lax.axis_index("dp")
        self.dp = dp
        self.x = dp // 2
        self.c = lax.rem(dp, 2)
        self.send_sem, self.recv_sem = send_sem, recv_sem
        self.used = 0
        self.unsent = []

    def at(self, axis):
        return {"z": self.z, "y": self.y, "x": self.x}[axis]

    def device(self, axis, position):
        z, y, x = self.z, self.y, self.x
        if axis == "z":
            z = position
        elif axis == "y":
            y = position
        else:
            x = position
        return (z, y, 2 * x + self.c)

    def sibling(self):
        return (self.z, self.y, 2 * self.x + 1 - self.c)

    def partner(self):
        return (self.z, self.y + 1 - 2 * lax.rem(self.y, 2), self.dp)

    def send(self, src, dst, device, landing=None):
        i = self.used
        self.used += 1
        copy = pltpu.make_async_remote_copy(
            src_ref=src,
            dst_ref=dst,
            send_sem=self.send_sem.at[i],
            recv_sem=self.recv_sem.at[i],
            device_id=device,
            device_id_type=MESH,
        )
        copy.start()
        self.unsent.append(copy)
        land = dst if landing is None else landing
        return pltpu.make_async_remote_copy(
            src_ref=land,
            dst_ref=land,
            send_sem=self.send_sem.at[i],
            recv_sem=self.recv_sem.at[i],
            device_id=device,
            device_id_type=MESH,
        ).wait_recv

    def drain(self):
        for copy in self.unsent:
            copy.wait_send()
        self.unsent = []


def run(generators, work=(), work_us=0.0):
    now = 0.0
    work = list(work)
    live = []
    for order, gen in enumerate(generators):
        live.append([next(gen), order, gen])
    while live:
        live.sort(key=lambda entry: entry[:2])
        entry = live[0]
        while work and entry[0] > now:
            work.pop(0)()
            now += work_us
        now = max(now, entry[0])
        try:
            entry[0] = now + next(entry[2])
        except StopIteration:
            live.pop(0)
    for item in work:
        item()


def wrap(position, n):
    return lax.rem(position + 2 * n, n)


def slab_index(comm, axis, position, free, lo, hi, half):
    index = {name: None if name in free else comm.at(name) for name in SIZE}
    index[axis] = position
    if half is not None:
        if free:
            name = free[0]
            count = SIZE[name] // 2
            index[name] = pl.ds(half * count, count)
        else:
            middle = lo + (hi - lo + 1) // 2
            lo, hi = (lo, middle) if half == 0 else (middle, hi)
    return tuple(whole(index[name]) for name in ("z", "y", "x")), lo, hi


def slab_bytes(axis, free, lo, hi, itemsize=2):
    count = 1
    for name in free:
        count *= SIZE[name]
    return count * (hi - lo) * TILE * LANES * itemsize


def gather_part(comm, held, lo, hi, order):
    landed = []

    def view(axis, position, free, half, core):
        (zi, yi, xi), a, b = slab_index(comm, axis, position, free, lo, hi, half)
        return held.at[zi, yi, xi, core, a:b]

    for phase, axis in enumerate(order):
        n, me = SIZE[axis], comm.at(axis)
        free = order[:phase]
        last = phase == 2
        right, left = comm.device(axis, wrap(me + 1, n)), comm.device(axis, wrap(me - 1, n))

        def share(position, half, free=free, axis=axis):
            src = view(axis, position, free, half, comm.c)
            landed.append(
                comm.send(src, src, comm.sibling(), landing=view(axis, position, free, half, 1 - comm.c))
            )

        us = slab_bytes(axis, free, lo, hi) / GBS + STEP_US
        for step in range(1, n // 2 + 1):
            ends = step == n // 2
            goes_right, goes_left = wrap(me - step + 1, n), wrap(me + step - 1, n)
            half_right, half_left = (0, 1) if ends else (None, None)
            src = view(axis, goes_right, free, half_right, comm.c)
            wait_left = comm.send(
                src, src, right, landing=view(axis, wrap(me - step, n), free, half_right, comm.c)
            )
            src = view(axis, goes_left, free, half_left, comm.c)
            wait_right = comm.send(
                src, src, left, landing=view(axis, wrap(me + step, n), free, half_left, comm.c)
            )
            if last:
                share(goes_right, None)
                if step > 1:
                    share(goes_left, None)
            yield us * (0.6 if ends else 1.0)
            wait_left()
            wait_right()
        if last:
            share(wrap(me - n // 2, n), 0)
            share(wrap(me + n // 2, n), 1)
    yield 3.0
    for wait in landed:
        wait()


def reduce_shapes():
    shapes = []
    for lo, hi, order in PARTS:
        axes = order[::-1]
        for phase, axis in enumerate(axes):
            free = axes[phase + 1 :]
            for step in range(SIZE[axis] // 2, 0, -1):
                ends = step == SIZE[axis] // 2
                for half in (0, 1):
                    dims = [SIZE[name] for name in ("z", "y", "x") if name in free]
                    tiles = hi - lo
                    if ends:
                        if free:
                            dims = [
                                SIZE[name] // (2 if name == free[0] else 1)
                                for name in ("z", "y", "x")
                                if name in free
                            ]
                        else:
                            tiles = (tiles + 1) // 2 if half == 0 else tiles // 2
                    shapes.append(
                        pltpu.VMEM((*dims, tiles, TILE, LANES), F32 if phase == 2 else BF16)
                    )
        shapes.append(pltpu.VMEM((SIZE[axes[2]], hi - lo, TILE, LANES), F32))
    return shapes


def reduce_part(comm, partial, result, lo, hi, order, buffers):
    axes = order[::-1]
    wide = buffers[-1]
    buffers = list(buffers[:-1])

    for phase, axis in enumerate(axes):
        n, me = SIZE[axis], comm.at(axis)
        free = axes[phase + 1 :]
        last = phase == 2
        right, left = comm.device(axis, wrap(me + 1, n)), comm.device(axis, wrap(me - 1, n))

        def view(position, half):
            if last:
                _, a, b = slab_index(comm, axis, position, (), lo, hi, half)
                return wide.at[position, a - lo : b - lo]
            (zi, yi, xi), a, b = slab_index(comm, axis, position, free, lo, hi, half)
            return partial.at[zi, yi, xi, comm.c, a:b]

        us = slab_bytes(axis, free, lo, hi, 4 if last else 2) / GBS + STEP_US + 0.3
        came = None
        for step in range(n // 2, 0, -1):
            ends = step == n // 2
            if came is not None:
                for side, (buffer, wait, half) in enumerate(came):
                    wait()
                    position = wrap(me + step, n) if side == 0 else wrap(me - step, n)
                    own = view(position, half)
                    total = own[...].astype(F32) + buffer[...].astype(F32)
                    own[...] = total.astype(own.dtype)
            came = []
            for side in (0, 1):
                half = side if ends else None
                position = wrap(me + step, n) if side == 0 else wrap(me - step, n)
                buffer = buffers.pop(0)
                wait = comm.send(view(position, half), buffer, right if side == 0 else left)
                came.append((buffer, wait, half))
            yield us * (0.6 if ends else 1.0)
        for _, wait, _ in came:
            wait()
        own = view(me, None)
        total = own[...].astype(F32) + came[0][0][...].astype(F32) + came[1][0][...].astype(F32)
        if last:
            result[lo:hi] = total
        elif phase == 1:
            wide[...] = total
        else:
            own[...] = total.astype(BF16)


def load_hidden(held, z):
    tiles = []
    for pair in (0, 1):
        even, odd = 2 * pair, 2 * pair + 1
        middle = jnp.concatenate([held[z, even, :, :, 7:11], held[z, odd, :, :, 0:3]], axis=2)
        for part in (held[z, even, :, :, 0:7], middle, held[z, odd, :, :, 3:10]):
            tiles.append(part.reshape(TOK, LANES))
    return jnp.concatenate(tiles, axis=1)


def kernel(
    own_ref, weight_ref, target_ref, onehot_ref, counts_ref, ref_ref, sign_ref, same_ref,
    logprobs_ref, hidden_grad_ref, weight_grad_ref,
    held, partial, padded, logits, dlogits, swap, stats, far, near, final, near_out, swapped,
    send_sem, recv_sem, local_sem, *buffers,
):
    comm = Comm(send_sem, recv_sem)
    even = lax.rem(comm.y, 2) == 0

    def weight_copy(i):
        return pltpu.make_async_copy(
            weight_ref.at[pl.ds(pl.multiple_of(i * PAIR, TILE), PAIR)],
            padded.at[pl.ds(pl.multiple_of(i * PADDED, TILE), PAIR)],
            local_sem.at[i],
        )

    for i in range(PAIRS):
        weight_copy(i).start()

    barrier = pltpu.get_barrier_semaphore()
    peers = []
    for axis, n in (("section", 8), ("tensor", 4), ("dp", 8)):
        me = lax.axis_index(axis)
        for offset in range(1, n):
            place = {"section": comm.z, "tensor": comm.y, "dp": comm.dp}
            place[axis] = lax.rem(me + offset, n)
            peers.append((place["section"], place["tensor"], place["dp"]))
    for peer in peers:
        pl.semaphore_signal(barrier, inc=1, device_id=peer, device_id_type=MESH)
    pl.semaphore_wait(barrier, len(peers))

    wait = comm.send(own_ref.at[1], swap, comm.partner())
    for i in range(PAIRS):
        padded[i * PADDED + PAIR : (i + 1) * PADDED] = jnp.zeros((PADDED - PAIR, COLS), BF16)
    wait()
    shared = own_ref[1] + swap[...]
    zero_tile = jnp.zeros((1, TILE, LANES), BF16)
    held[comm.z, comm.y, comm.x, comm.c] = jnp.where(
        even,
        jnp.concatenate([own_ref[0], shared[0:4]], axis=0),
        jnp.concatenate([shared[4:7], own_ref[0], zero_tile], axis=0),
    )

    run([gather_part(comm, held, lo, hi, order) for lo, hi, order in PARTS])

    for i in range(PAIRS):
        weight_copy(i).wait()

    logits[...] = jnp.zeros_like(logits)

    @pl.loop(0, 8)
    def _(z):
        logits[...] += jnp.dot(
            load_hidden(held, z),
            padded[pl.ds(pl.multiple_of(z * 2 * PADDED, LANES), 2 * PADDED)],
            preferred_element_type=F32,
        )

    first = ((comm.z * 4 + comm.y) * 8 + comm.dp) * COLS
    columns = first + lax.broadcasted_iota(jnp.int32, (LANES, COLS), 1)
    lane = lax.broadcasted_iota(jnp.int32, (LANES, LANES), 1)
    stats[...] = jnp.zeros_like(stats)
    for j in range(TOK // LANES):
        rows = slice(j * LANES, (j + 1) * LANES)
        block = logits[rows]
        top = jnp.max(block, axis=1, keepdims=True)
        total = jnp.sum(jnp.exp(block - top), axis=1, keepdims=True)
        picked = jnp.sum(jnp.where(target_ref[rows] == columns, block, 0.0), axis=1, keepdims=True)
        turned = jnp.where(lane == 0, top, jnp.where(lane == 1, total, picked)).T
        for i in range(3):
            stats[i, j : j + 1] = turned[i : i + 1]

    for axis, n, slots in (("dp", 8, far.at[0]), ("tensor", 4, near), ("section", 8, far.at[1])):
        me = lax.axis_index(axis)
        waits = []
        slots[me] = stats[...]
        for offset in range(1, n):
            place = {"section": comm.z, "tensor": comm.y, "dp": comm.dp}
            place[axis] = lax.rem(me + offset, n)
            waits.append(
                comm.send(
                    slots.at[me],
                    slots.at[me],
                    (place["section"], place["tensor"], place["dp"]),
                    landing=slots.at[lax.rem(me + n - offset, n)],
                )
            )
        for wait in waits:
            wait()
        tops = [slots[i, 0] for i in range(n)]
        top = tops[0]
        for i in range(1, n):
            top = jnp.maximum(top, tops[i])
        total = slots[0, 1] * jnp.exp(tops[0] - top)
        picked = slots[0, 2]
        for i in range(1, n):
            total += slots[i, 1] * jnp.exp(tops[i] - top)
            picked += slots[i, 2]
        stats[0] = top
        stats[1] = total
        stats[2] = picked
        comm.drain()

    log_total = stats[0] + jnp.log(jnp.where(stats[1] > 0.0, stats[1], 1.0))
    terms = stats[2] - log_total
    row = jnp.concatenate([terms[j : j + 1] for j in range(TOK // LANES)], axis=1)
    counts = counts_ref[...]
    sign = sign_ref[...]
    logprobs = jnp.sum(onehot_ref[...] * row, axis=1, keepdims=True) / counts
    logprobs_ref[...] = logprobs
    contrib = sign * (logprobs - ref_ref[...])
    seq = (16, 16)
    eye = lax.broadcasted_iota(jnp.int32, seq, 0) == lax.broadcasted_iota(jnp.int32, seq, 1)
    across = jnp.sum(jnp.where(eye, contrib, 0.0), axis=0, keepdims=True)
    margin = jnp.sum(same_ref[...] * across, axis=1, keepdims=True)
    coefficient = -loss_scale * beta_value * jax.nn.sigmoid(-beta_value * margin) * sign
    token_weight = jnp.sum(onehot_ref[...] * (coefficient / counts), axis=0, keepdims=True)

    for j in range(TOK // LANES):
        rows = slice(j * LANES, (j + 1) * LANES)
        log_column = jnp.broadcast_to(log_total[j : j + 1], (LANES, LANES)).T[:, 0:1]
        weight_column = jnp.broadcast_to(token_weight[:, rows], (LANES, LANES)).T[:, 0:1]
        probs = jnp.exp(logits[rows] - log_column)
        hit = (target_ref[rows] == columns).astype(F32)
        dlogits[rows] = (weight_column * (hit - probs)).astype(BF16)

    def core_copy(z):
        return pltpu.make_async_remote_copy(
            src_ref=partial.at[z, :, :, 1 - comm.c],
            dst_ref=near_out.at[z],
            send_sem=send_sem.at[comm.used + z],
            recv_sem=recv_sem.at[comm.used + z],
            device_id=comm.sibling(),
            device_id_type=MESH,
        )

    @pl.loop(0, 8)
    def _(z):
        for pair in (0, 1):
            terms = lax.dot_general(
                dlogits[...],
                padded[pl.ds(pl.multiple_of((2 * z + pair) * PADDED, LANES), PADDED)],
                (((1,), (1,)), ((), ())),
                preferred_element_type=F32,
            ).astype(BF16)
            left, middle, right = (
                terms[:, i * LANES : (i + 1) * LANES].reshape(4, 2, 7, TILE, LANES) for i in range(3)
            )
            partial[z, 2 * pair, :, :, 0:7] = left
            partial[z, 2 * pair, :, :, 7:11] = middle[:, :, 0:4]
            partial[z, 2 * pair + 1, :, :, 0:3] = middle[:, :, 4:7]
            partial[z, 2 * pair + 1, :, :, 3:10] = right
            partial[z, 2 * pair + 1, :, :, 10:11] = jnp.zeros((4, 2, 1, TILE, LANES), BF16)
        core_copy(z).start()

    @pl.loop(0, 8)
    def _(z):
        core_copy(z).wait()
        for y in range(4):
            mine = partial[z, y, :, comm.c].astype(F32) + near_out[z, y].astype(F32)
            partial[z, y, :, comm.c] = mine.astype(BF16)

    comm.used += 8

    def grad_copy(i):
        return pltpu.make_async_copy(
            padded.at[pl.ds(pl.multiple_of(i * PADDED, TILE), PAIR)],
            weight_grad_ref.at[pl.ds(pl.multiple_of(i * PAIR, TILE), PAIR)],
            local_sem.at[i],
        )

    def weight_grad(z):
        def item():
            features = load_hidden(held, z)
            block = lax.dot_general(
                features, dlogits[...], (((0,), (0,)), ((), ())), preferred_element_type=F32
            )
            padded[z * 2 * PADDED : (z + 1) * 2 * PADDED] = block.astype(BF16)
            grad_copy(2 * z).start()
            grad_copy(2 * z + 1).start()

        return item

    generators, taken = [], 0
    for lo, hi, order in PARTS:
        count = 2 * sum(SIZE[axis] // 2 for axis in order) + 1
        generators.append(
            reduce_part(comm, partial, final, lo, hi, order, buffers[taken : taken + count])
        )
        taken += count
    run(generators, [weight_grad(z) for z in range(8)], 1.0)

    mine = final[...].astype(BF16)
    near_send = swap.at[0:4]
    swap[0:4] = jnp.where(even, mine[7:11], jnp.concatenate([mine[0:3], mine[0:1]], axis=0))
    comm.drain()
    comm.send(near_send, swapped, comm.partner())()
    other = swapped[...]
    hidden_grad_ref[0] = jnp.where(even, mine[0:7], mine[3:10])
    hidden_grad_ref[1] = jnp.where(
        even,
        jnp.concatenate([mine[7:11], other[0:3]], axis=0),
        jnp.concatenate([other, mine[0:3]], axis=0),
    )
    comm.drain()
    for i in range(PAIRS):
        grad_copy(i).wait()


def per_device(hidden, head_weight, targets, response_mask, pair_ids, ref_logprobs):
    even = lax.rem(lax.axis_index("tensor"), 2) == 0
    plain = jnp.pad(hidden, ((0, 0), (0, 88)))
    moved = jnp.pad(hidden, ((0, 0), (40, 48)))
    own = jnp.stack(
        [
            jnp.where(even, plain[:, :LANES], moved[:, LANES:]),
            jnp.where(even, plain[:, LANES:], moved[:, :LANES]),
        ]
    ).reshape(2, 7, TILE, LANES)

    seqs = pair_ids.shape[0]
    mask = response_mask.astype(F32)
    onehot = jnp.where(
        jnp.arange(TOK)[None, :] // (TOK // seqs) == jnp.arange(seqs)[:, None], mask[None, :], 0.0
    )
    counts = jnp.sum(onehot, axis=1, keepdims=True)
    same = pair_ids[:, None] == pair_ids[None, :]
    index = jnp.arange(seqs, dtype=jnp.int32)
    earlier = jnp.sum((same & (index[None, :] < index[:, None])).astype(jnp.int32), axis=1, keepdims=True)
    sign = jnp.where(earlier == 0, 1.0, -1.0).astype(F32)

    vmem = pl.BlockSpec(memory_space=pltpu.VMEM)
    hbm = pl.BlockSpec(memory_space=pl.ANY)
    copies = 160
    logprobs, parts, grad_weight = pl.pallas_call(
        kernel,
        out_shape=(
            jax.ShapeDtypeStruct((seqs, 1), F32),
            jax.ShapeDtypeStruct((2, 7, TILE, LANES), BF16),
            jax.ShapeDtypeStruct(head_weight.shape, BF16),
        ),
        in_specs=[vmem, hbm, vmem, vmem, vmem, vmem, vmem, vmem],
        out_specs=(vmem, vmem, hbm),
        scratch_shapes=[
            pltpu.VMEM((8, 4, 4, 2, BLOB, TILE, LANES), BF16),
            pltpu.VMEM((8, 4, 4, 2, BLOB, TILE, LANES), BF16),
            pltpu.VMEM((PAIRS * PADDED, COLS), BF16),
            pltpu.VMEM((TOK, COLS), F32),
            pltpu.VMEM((TOK, COLS), BF16),
            pltpu.VMEM((7, TILE, LANES), BF16),
            pltpu.VMEM((3, 8, LANES), F32),
            pltpu.VMEM((2, 8, 3, 8, LANES), F32),
            pltpu.VMEM((4, 3, 8, LANES), F32),
            pltpu.VMEM((BLOB, TILE, LANES), F32),
            pltpu.VMEM((8, 4, 4, BLOB, TILE, LANES), BF16),
            pltpu.VMEM((4, TILE, LANES), BF16),
            pltpu.SemaphoreType.DMA((copies,)),
            pltpu.SemaphoreType.DMA((copies,)),
            pltpu.SemaphoreType.DMA((PAIRS,)),
            *reduce_shapes(),
        ],
        compiler_params=pltpu.CompilerParams(
            collective_id=0, has_side_effects=True, vmem_limit_bytes=60 * 1024 * 1024
        ),
        cost_estimate=pl.CostEstimate(
            flops=6 * TOK * 5376 * COLS, bytes_accessed=12 * 1024 * 1024, transcendentals=2 * TOK * COLS
        ),
    )(
        own, head_weight, targets[:, None], onehot, counts, ref_logprobs[:, None], sign, same.astype(F32)
    )

    tile, shared = parts[0].reshape(ROWS, LANES), parts[1].reshape(ROWS, LANES)
    grad_hidden = jnp.where(
        even,
        jnp.concatenate([tile, shared[:, :40]], axis=1),
        jnp.concatenate([shared[:, 40:], tile[:, :80]], axis=1),
    )
    return (logprobs[:, 0], grad_hidden, grad_weight)


def solution(mesh):
    placed = (
        P("dp", ("section", "tensor")),
        P(None, ("section", "tensor", "dp")),
        P(),
        P(),
        P(),
        P(),
    )
    return jax.shard_map(
        per_device,
        mesh=mesh,
        in_specs=placed,
        out_specs=(P(), P("dp", ("section", "tensor")), P(None, ("section", "tensor", "dp"))),
        check_vma=False,
    )
```

time: 593 us -> 165 us (0.28)
  waiting for transfers between devices: 367 us -> 0 us
  blocking collectives: 162 us -> 0 us
  Pallas kernels: 0 us -> 146 us
  matrix products: 34.8 us -> 0 us
  between operations: 13.9 us -> 0.69 us
    unnamed x5 -> x0, waiting for transfers between devices: 261 us -> none
    pallas_call x0 -> x1, Pallas kernels: none -> 146 us  [per_device(): pl.pallas_call(kernel, out_shape=(jax.ShapeDtypeStruct((seqs, 1), F32), j...]
    all_gather x1 -> x0, waiting for transfers between devices: 105 us -> none  [per_device(): lax.all_gather(partial_value, ('section', 'tensor'), axis=1, tiled=True)]
    pmax x1 -> x0, blocking collectives: 75.2 us -> none  [per_device(): row_top = lax.pmax(local_top, ('section', 'tensor', 'dp'))]
    psum x1 -> x0, blocking collectives: 73.5 us -> none  [per_device(): lax.psum((local_total, picked), ('section', 'tensor', 'dp'))]
    dot_general x3 -> x0, matrix products: 34.8 us -> none  [the longest x1 12.3 us: per_device(): lax.dot_general(dlogits, head_weight, (((1,), (1,)), ((), ())), preferred...]
    all_gather x1 -> x0, blocking collectives: 13.5 us -> none  [per_device(): partial_value = lax.all_gather(hidden, 'dp', axis=0, tiled=True)]
    unnamed x12 -> x3, local copies, waits for them, and re-layouts: 13.2 us -> 5.54 us
  transfers between devices with their start and end apart: 3 -> 0, of which waited for: 3 -> 0; matrix products, arithmetic and copies ran while one was open for 3% -> 0% of each run, Pallas kernels for 0% -> 0%
where the time goes in v1:
time: 165 us
  Pallas kernels  146 us (88%)
  local copies, waits for them, and re-layouts  11.1 us (7%)
  other arithmetic  7.18 us (4%)
    pallas_call x1, Pallas kernels, per_device(): pl.pallas_call(kernel, out_shape=(jax.ShapeDtypeStruct((seqs, 1), F32), j...  146 us
    unnamed x3, local copies, waits for them, and re-layouts  5.54 us

profile of v1, /device:TPU:8, one launch (start us, length us, event | category | flops | bytes accessed | tf_op | source)
XLA Modules:
  0.0 164.6 jit_solution(10764861694540425141)
XLA Ops:
  0.6 0.9 convert_reduce_fusion
  1.6 0.7 convert_element_type.13
  2.3 0.7 copy.23.sign_ref
  2.9 1.3 copy.22.ref_ref
  4.3 1.4 compare_convert_fusion.same_ref
  5.7 0.7 fusion.3
  6.4 0.7 copy.21.counts_ref
  7.1 0.8 fusion.2
  7.9 0.1 copy.18
  8.0 0.1 copy.19
  8.1 0.6 pad_maximum_fusion.own_ref
  8.8 1.6 broadcast_in_dim.44.target_ref
  10.4 145.7 %shard_map.85 = (f32[16,1]{1,0:T(8,128)}, bf16[2,7,16,128]{3,2,1,0:T(8,128)(2,1)}, bf16[5376,512]{1,0:T(8,128)(2,1)}) custom-call(bf16[2,7,16,128]{3,2,1,0:T(8,128)(2,1)} %pad_maximum_fusion.own_ref, bf16[5376,512]{1,0:T(8,128)(2,1)} %weight_ref.1, s32[896,1]{1,0:T(8,128)} %broadcast_in_dim.44.target_ref, f32[16,896]{1,0:T(8,128)} %get-tuple-element.14.onehot_ref, ...), custom_call_target="tpu_custom_call" | custom-call | flops 14797504512 | bytes 12582912 | tf_op jit(solution)/shard_map/pallas_call | solution.py:510
  156.1 1.3 reduce
  157.4 0.8 fusion.8
  158.2 0.1 copy.25
  158.3 0.1 copy.28
  158.4 0.1 slice.38
  158.5 0.1 copy.29
  158.6 0.6 maximum_select_fusion
  159.3 5.4 %copy.31 = bf16[5376,512]{1,0:T(8,128)(2,1)} copy(bf16[5376,512]{1,0:T(8,128)(2,1)} %get-tuple-element.20) | data formatting | bytes 11010048
  (3 shorter events, 0.0 us)
